TPU v7x, 32 devices: a whole 2x2x4 slice. The times are simulated.
32 devices in a mesh: tile: 4 (over y, x), box: 4 (over z), slab: 2 (over core).
Axes of the slice: x: 2, y: 2, z: 4, core: 2. Of those that a mesh axis runs over, the one named last changes fastest.
Arguments:
- les: bfloat16 [1024, 3, 48, 256], P(('tile', 'box'), None, 'slab'), may hold values from -6 to 6
- tile_owner: int32 [80, 25, 1], replicated, may hold values from 0 to 15; in each aligned block of 125 rows (0 to 124, 125 to 249, ..., all dimensions but the last counted through in order) at most 9 rows name the same one
- tile_slot: int32 [80, 25], replicated, may hold values from 0 to 63
- box_offset: int32 [80, 2], P(('tile', 'box')), may hold values from 0 to 127
- plane_deficit: float32 [64, 64, 64], P(('tile', 'box'), 'slab'), may hold values from -2.4 to 2.4
- plane_box: int32 [64, 4], P(('tile', 'box')), may hold values from 0 to 79, as said below
- plane_weight: float32 [64, 4], P(('tile', 'box')), may hold values from 0.5 to 1.5
Outputs:
- inflow: bfloat16 [80, 3, 64, 4096], P(('tile', 'box'), None, 'slab')
Inputs may be any that keep to these rules, and one draw needn't show every extreme that they name: tile_owner[b, q, 0] is the device along tile+box that holds patch tile q of box b; over the 125 rows of the boxes of one owner no device is named more than 9 times. `plane_box`: box b belongs to owner b // 5; the 4 boxes of one plane have different owners, and over the planes held by one index of tile+box no owner is named more than 1 times, some owner exactly 1 times.
All inputs are finite; a program needn't handle non-finite values.
Results may differ from a plain program's by a relative error of at most 0.0039.
Values may be sent and summed in bfloat16 or wider, within the bound.
A program may use at most 128 MiB of HBM per device.

v0:
```python
import jax
import jax.numpy as jnp
from jax import lax
from jax.sharding import PartitionSpec as P

BOXN = 64
TS = 16
LZ = 48
FILTER_NU = 0.125


def padded(x, sides, width):
    for axis, dim in sides:
        size, length = (lax.axis_size(axis), x.shape[dim])
        up = [(i, (i + 1) % size) for i in range(size - 1)]
        down = [(j, i) for i, j in up]
        last = lax.slice_in_dim(x, length - width, length, axis=dim)
        initial = lax.slice_in_dim(x, 0, width, axis=dim)
        before = lax.ppermute(last, axis, up)
        after = lax.ppermute(initial, axis, down)
        x = jnp.concatenate([before, x, after], axis=dim)
    return x


def blend_weights(shift, share, width):
    grid = jnp.arange(width, dtype=jnp.int32)[:, None]
    target = shift + jnp.arange(BOXN, dtype=jnp.int32)[None, :]
    lower = (grid == target).astype(jnp.float32) * (1.0 - share)
    upper = (grid == target + 1).astype(jnp.float32) * share
    return lower + upper


def body(les, tile_owner, tile_slot, box_offset, plane_deficit, plane_box, plane_weight):
    owners = lax.axis_size(("tile", "box"))
    my_index = lax.axis_index(("tile", "box"))
    slab_index = lax.axis_index("slab")
    slab_levels = les.shape[2]
    patch_count = tile_owner.shape[1]
    patch_side = BOXN // TS + 1
    width = patch_side * TS
    box_count = box_offset.shape[0]
    need_count = box_count * patch_count
    slot_count = (need_count + owners - 1) // owners + 1
    sources = tile_owner[:, :, 0].reshape(owners, need_count)
    local_tiles = tile_slot.reshape(owners, need_count)
    from_here = (sources == my_index).astype(jnp.int32)
    slot_rank = jnp.cumsum(from_here, axis=1) - from_here
    slot_ids = jnp.arange(slot_count, dtype=jnp.int32)
    chosen = (from_here[:, None, :] == 1) & (slot_rank[:, None, :] == slot_ids[None, :, None])
    picked = jnp.sum(jnp.where(chosen, local_tiles[:, None, :], 0), axis=2).reshape(-1)
    band_tiles = padded(les, (("slab", 2),), 1)
    outgoing = jnp.take(band_tiles, picked, axis=0)
    incoming = lax.all_to_all(outgoing, ("tile", "box"), split_axis=0, concat_axis=0, tiled=True)
    wanted = lax.dynamic_slice_in_dim(sources, my_index, 1, 0)[0]
    need_ids = jnp.arange(need_count, dtype=jnp.int32)
    same_source = (wanted[:, None] == wanted[None, :]) & (need_ids[None, :] < need_ids[:, None])
    slot_of = jnp.sum(same_source.astype(jnp.int32), axis=1)
    flat_index = (wanted * slot_count + slot_of).reshape(box_count, patch_count)
    slab_points = plane_deficit.shape[1]
    plane_count, contrib_count = plane_box.shape
    deficit_terms = (plane_weight[:, :, None, None] * plane_deficit[:, None, :, :]).reshape(
        plane_count * contrib_count, -1
    )
    box_total = owners * box_count
    onehot = (plane_box.reshape(1, -1) == jnp.arange(box_total, dtype=jnp.int32)[:, None]).astype(
        jnp.float32
    )
    partial_value = jnp.dot(
        onehot, deficit_terms, precision=lax.Precision.HIGHEST, preferred_element_type=jnp.float32
    )
    summed = lax.psum(partial_value, ("tile", "box"))
    wake_loss = lax.dynamic_slice_in_dim(summed, my_index * box_count, box_count, 0)
    wake_loss = wake_loss.reshape(box_count, slab_points, BOXN)
    points = slab_index * slab_points + jnp.arange(slab_points, dtype=jnp.int32)
    level_num = points * (LZ - 1)
    level_low = level_num // (BOXN - 1) - slab_index * slab_levels + 1
    level_frac = (level_num % (BOXN - 1)).astype(jnp.float32) / float(BOXN - 1)
    level_count = incoming.shape[2]
    level_grid = jnp.arange(level_count, dtype=jnp.int32)[:, None]
    height_weights = (level_grid == level_low[None, :]).astype(jnp.float32) * (
        1.0 - level_frac[None, :]
    )
    height_weights = (
        height_weights
        + (level_grid == level_low[None, :] + 1).astype(jnp.float32) * level_frac[None, :]
    )

    def one_box(packed):
        box_ids, offset, box_loss = packed
        patch_tiles = jnp.take(incoming, box_ids, axis=0)
        patch_tiles = patch_tiles.reshape(patch_side, patch_side, 3, level_count, TS, TS)
        share_x = (offset[0] % 8).astype(jnp.float32) / 8.0
        share_y = (offset[1] % 8).astype(jnp.float32) / 8.0
        weights_x = (
            blend_weights(offset[0] // 8, share_x, width)
            .reshape(patch_side, TS, BOXN)
            .astype(jnp.bfloat16)
        )
        weights_y = blend_weights(offset[1] // 8, share_y, width).reshape(patch_side, TS, BOXN)
        along_x = jnp.einsum(
            "rscLyx,sxi->cLryi", patch_tiles, weights_x, preferred_element_type=jnp.float32
        )
        along_y = jnp.einsum(
            "cLryi,ryj->cLji",
            along_x,
            weights_y,
            precision=lax.Precision.HIGHEST,
            preferred_element_type=jnp.float32,
        )
        along_y = along_y.reshape(3, level_count, BOXN * BOXN)
        velocity = jnp.einsum(
            "cLp,Lk->ckp",
            along_y,
            height_weights,
            precision=lax.Precision.HIGHEST,
            preferred_element_type=jnp.float32,
        )
        velocity = velocity.reshape(3, slab_points, BOXN, BOXN)
        velocity = velocity.at[0].add(-box_loss[:, :, None])
        return velocity.astype(jnp.bfloat16).reshape(3, slab_points, BOXN * BOXN)

    box_flow = lax.map(one_box, (flat_index, box_offset, wake_loss))
    extended = padded(box_flow, (("slab", 2),), 1).astype(jnp.float32)
    center = extended[:, :, 1:-1]
    depth = points[None, None, :, None]
    lower_plane = jnp.where(depth == 0, center, extended[:, :, :-2])
    upper_plane = jnp.where(depth == BOXN - 1, center, extended[:, :, 2:])
    column = jnp.arange(BOXN * BOXN, dtype=jnp.int32) % BOXN
    prior_row = jnp.concatenate([center[..., :BOXN], center[..., :-BOXN]], axis=3)
    next_row = jnp.concatenate([center[..., BOXN:], center[..., -BOXN:]], axis=3)
    prior_col = jnp.where(
        column == 0, center, jnp.concatenate([center[..., :1], center[..., :-1]], axis=3)
    )
    next_col = jnp.where(
        column == BOXN - 1, center, jnp.concatenate([center[..., 1:], center[..., -1:]], axis=3)
    )
    stencil_sum = lower_plane - center + (upper_plane - center)
    stencil_sum = stencil_sum + (prior_row - center) + (next_row - center)
    stencil_sum = stencil_sum + (prior_col - center) + (next_col - center)
    return (center + FILTER_NU * stencil_sum).astype(jnp.bfloat16)


def solution(mesh):
    placed = (
        P(("tile", "box"), None, "slab", None),
        P(),
        P(),
        P(("tile", "box"), None),
        P(("tile", "box"), "slab", None),
        P(("tile", "box"), None),
        P(("tile", "box"), None),
    )
    return jax.shard_map(
        body,
        mesh=mesh,
        in_specs=placed,
        out_specs=P(("tile", "box"), None, "slab", None),
        check_vma=False,
    )
```

profile of v0, /device:TPU:0, one launch (start us, length us, event | category | flops | bytes accessed | tf_op | source)
XLA Modules:
  0.0 487.5 jit_solution(6979024093422560494)
XLA Ops:
  15.6 3.9 pad_maximum_fusion
  19.4 8.9 %gather_fusion.1 = bf16[144,3,26,256]{3,2,1,0:T(8,128)(2,1)} fusion(bf16[64,3,26,256]{3,2,1,0:T(8,128)(2,1)S(1)} %pad_maximum_fusion, s32[1024]{0:T(1024)S(1)} %pad_clamp_fusion.1), kind=kCustom, calls=%fused_computation.1 | custom fusion | bytes 11502144 | tf_op jit(solution)/shard_map/jit(_take)/gather | solution.py:52
  28.4 6.6 %broadcast_select_fusion.1 = bf16[144,3,26,256]{3,2,1,0:T(8,128)(2,1)} fusion(bf16[144,3,26,256]{3,2,1,0:T(8,128)(2,1)} %gather_fusion.1, pred[144]{0:T(512)(128)(4,1)S(1)} %compare_and_fusion.1), kind=kLoop, calls=%fused_computation.74 | loop fusion | flops 2875392 | bytes 11501712 | tf_op jit(solution)/shard_map/jit(_take)/select_n | solution.py:52
  35.0 8.5 %all-to-all-start = ((bf16[144,3,26,256]{3,2,1,0:T(8,128)(2,1)}), bf16[144,3,26,256]{3,2,1,0:T(8,128)(2,1)}, u32[]{:S(2)}, u32[]{:S(2)}) async-start(bf16[144,3,26,256]{3,2,1,0:T(8,128)(2,1)} %broadcast_select_fusion.1), calls=%async_computation | async-start | bytes 14155776 | tf_op jit(solution)/shard_map/all_to_all | solution.py:53
  45.9 211.5 %all-reduce.2.cloned.1.call-done = f32[80,2048]{1,0:T(8,128)} async-done(((f32[80,2048]{1,0:T(8,128)}), f32[80,2048]{1,0:T(8,128)}) %all-reduce.2.cloned.1.call-update) | async-done | bytes 655376 | tf_op jit(solution)/shard_map/psum | solution.py:71
  258.4 181.3 %while.15 = (s32[]{:T(128)}, bf16[5,3,32,4096]{3,2,1,0:T(8,128)(2,1)}, s32[5,2]{0,1:T(2,128)S(1)}, s32[5,25]{1,0:T(8,128)S(1)}, bf16[144,3,26,256]{3,2,1,0:T(8,1...) while((s32[]{:T(128)}, ...), condition=%wide.region_5.6_spmd.clone, body=%wide.region_4.5_spmd.clone.sunk | while | flops 493983968 | bytes 24612900 | solution.py:122
  264.5 3.6 gather_fusion
  268.1 6.9 %gather.24 = bf16[5,5,3,26,16,16]{5,4,3,2,1,0:T(8,128)(2,1)} reshape(bf16[25,3,26,256]{3,2,1,0:T(8,128)(2,1)S(1)} %gather_fusion) | data formatting | bytes 1996800 | tf_op jit(solution)/shard_map/while/body/eval_jaxpr/jit(_take)/gather | solution.py:90
  275.0 5.6 %fusion.96 = f32[64,5,3,26,16,1]{0,4,5,1,3,2:T(8,128)S(1)} fusion(f32[]{:T(128)S(6)} %div.72, s32[64]{0:T(128)S(1)} %get-tuple-element.283, f32[]{:T(128)S(6)} %sub.148, s32[64]{0:T(128)S(1)} %get-tuple-element.284, s32[5,16]{1,0:T(8,128)S(1)} %multiply_add_fusion.2, bf16[5,5,3,26,16,16]{5,4,3,2,1,0:T(8,128)(2,1)} %gather.24, ...), kind=kOutput, calls=%fused_computation.3.clone.1 | convolution fusion | flops 64427520 | bytes 2596705 | tf_op jit(solution)/shard_map/while/body/eval_jaxpr/rscLyx,sxi->cLryi/dot_general | solution.py:100
  300.7 3.6 gather_fusion
  304.3 6.9 %gather.24 = bf16[5,5,3,26,16,16]{5,4,3,2,1,0:T(8,128)(2,1)} reshape(bf16[25,3,26,256]{3,2,1,0:T(8,128)(2,1)S(1)} %gather_fusion) | data formatting | bytes 1996800 | tf_op jit(solution)/shard_map/while/body/eval_jaxpr/jit(_take)/gather | solution.py:90
  311.2 5.6 %fusion.96 = f32[64,5,3,26,16,1]{0,4,5,1,3,2:T(8,128)S(1)} fusion(f32[]{:T(128)S(6)} %div.72, s32[64]{0:T(128)S(1)} %get-tuple-element.283, f32[]{:T(128)S(6)} %sub.148, s32[64]{0:T(128)S(1)} %get-tuple-element.284, s32[5,16]{1,0:T(8,128)S(1)} %multiply_add_fusion.2, bf16[5,5,3,26,16,16]{5,4,3,2,1,0:T(8,128)(2,1)} %gather.24, ...), kind=kOutput, calls=%fused_computation.3.clone.1 | convolution fusion | flops 64427520 | bytes 2596705 | tf_op jit(solution)/shard_map/while/body/eval_jaxpr/rscLyx,sxi->cLryi/dot_general | solution.py:100
  337.0 3.6 gather_fusion
  340.6 6.9 %gather.24 = bf16[5,5,3,26,16,16]{5,4,3,2,1,0:T(8,128)(2,1)} reshape(bf16[25,3,26,256]{3,2,1,0:T(8,128)(2,1)S(1)} %gather_fusion) | data formatting | bytes 1996800 | tf_op jit(solution)/shard_map/while/body/eval_jaxpr/jit(_take)/gather | solution.py:90
  347.5 5.6 %fusion.96 = f32[64,5,3,26,16,1]{0,4,5,1,3,2:T(8,128)S(1)} fusion(f32[]{:T(128)S(6)} %div.72, s32[64]{0:T(128)S(1)} %get-tuple-element.283, f32[]{:T(128)S(6)} %sub.148, s32[64]{0:T(128)S(1)} %get-tuple-element.284, s32[5,16]{1,0:T(8,128)S(1)} %multiply_add_fusion.2, bf16[5,5,3,26,16,16]{5,4,3,2,1,0:T(8,128)(2,1)} %gather.24, ...), kind=kOutput, calls=%fused_computation.3.clone.1 | convolution fusion | flops 64427520 | bytes 2596705 | tf_op jit(solution)/shard_map/while/body/eval_jaxpr/rscLyx,sxi->cLryi/dot_general | solution.py:100
  376.8 6.9 %gather.24 = bf16[5,5,3,26,16,16]{5,4,3,2,1,0:T(8,128)(2,1)} reshape(bf16[25,3,26,256]{3,2,1,0:T(8,128)(2,1)S(1)} %gather_fusion) | data formatting | bytes 1996800 | tf_op jit(solution)/shard_map/while/body/eval_jaxpr/jit(_take)/gather | solution.py:90
  383.7 5.6 %fusion.96 = f32[64,5,3,26,16,1]{0,4,5,1,3,2:T(8,128)S(1)} fusion(f32[]{:T(128)S(6)} %div.72, s32[64]{0:T(128)S(1)} %get-tuple-element.283, f32[]{:T(128)S(6)} %sub.148, s32[64]{0:T(128)S(1)} %get-tuple-element.284, s32[5,16]{1,0:T(8,128)S(1)} %multiply_add_fusion.2, bf16[5,5,3,26,16,16]{5,4,3,2,1,0:T(8,128)(2,1)} %gather.24, ...), kind=kOutput, calls=%fused_computation.3.clone.1 | convolution fusion | flops 64427520 | bytes 2596705 | tf_op jit(solution)/shard_map/while/body/eval_jaxpr/rscLyx,sxi->cLryi/dot_general | solution.py:100
  409.4 3.6 gather_fusion
  413.1 6.9 %gather.24 = bf16[5,5,3,26,16,16]{5,4,3,2,1,0:T(8,128)(2,1)} reshape(bf16[25,3,26,256]{3,2,1,0:T(8,128)(2,1)S(1)} %gather_fusion) | data formatting | bytes 1996800 | tf_op jit(solution)/shard_map/while/body/eval_jaxpr/jit(_take)/gather | solution.py:90
  419.9 5.6 %fusion.96 = f32[64,5,3,26,16,1]{0,4,5,1,3,2:T(8,128)S(1)} fusion(f32[]{:T(128)S(6)} %div.72, s32[64]{0:T(128)S(1)} %get-tuple-element.283, f32[]{:T(128)S(6)} %sub.148, s32[64]{0:T(128)S(1)} %get-tuple-element.284, s32[5,16]{1,0:T(8,128)S(1)} %multiply_add_fusion.2, bf16[5,5,3,26,16,16]{5,4,3,2,1,0:T(8,128)(2,1)} %gather.24, ...), kind=kOutput, calls=%fused_computation.3.clone.1 | convolution fusion | flops 64427520 | bytes 2596705 | tf_op jit(solution)/shard_map/while/body/eval_jaxpr/rscLyx,sxi->cLryi/dot_general | solution.py:100
  439.7 4.5 copy.42
  451.1 7.2 %fusion.71 = (f32[5,3,32,4095]{3,2,1,0:T(8,128)}, f32[5,3,32,4095]{3,2,1,0:T(8,128)}) fusion(f32[5,3,34,4096]{3,2,1,0:T(8,128)S(1)} %maximum_convert_fusion), kind=kLoop, calls=%fused_computation.123 | loop fusion | bytes 31449600 | tf_op jit(solution)/shard_map/slice | solution.py:135
  458.3 7.1 %fusion.72 = (f32[5,3,32,4032]{3,2,1,0:T(8,128)}, f32[5,3,32,4032]{3,2,1,0:T(8,128)}) fusion(f32[5,3,34,4096]{3,2,1,0:T(8,128)S(1)} %maximum_convert_fusion), kind=kLoop, calls=%fused_computation.124 | loop fusion | bytes 30965760 | tf_op jit(solution)/shard_map/slice | solution.py:130
  465.4 15.3 %fusion.50 = bf16[5,3,32,4096]{3,2,1,0:T(8,128)(2,1)} fusion(f32[5,3,34,4096]{3,2,1,0:T(8,128)S(1)} %maximum_convert_fusion, f32[5,3,32,4032]{3,2,1,0:T(8,128)} %get-tuple-element.196, f32[5,3,32,64]{3,2,1,0:T(8,128)S(1)} %get-tuple-element.202, f32[5,3,32,64]{3,2,1,0:T(8,128)S(1)} %get-tuple-element.201, f32[5,3,32,4032]{3,2,1,0:T(8,128)} %get-tuple-element.195, ...), kind=kLoop, calls=%fused_computation.71 | loop fusion | flops 43253760 | bytes 58990656 | tf_op jit(solution)/shard_map/convert_element_type | solution.py:140
  (164 shorter events, 96.8 us)
Async XLA Ops:
  8.2 7.0 %collective-permute-start.1 = (bf16[64,3,1,256]{3,0,2,1:T(8,128)(2,1)S(1)}, bf16[64,3,1,256]{3,0,2,1:T(8,128)(2,1)S(1)}, u32[]{:S(2)}, u32[]{:S(2)}) collective-permute-start(bf16[64,3,1,256]{3,0,2,1:T(8,128)(2,1)S(1)} %copy.51), channel_id=1, source_target_pairs={{1,0},{3,2},{5,4},{7,6},{9,8},{11,10},{13,12},{15,14},{17,16},{19,... | collective-permute-start | bytes 294920 | tf_op jit(solution)/shard_map/ppermute | solution.py:20
  9.6 5.8 %collective-permute-start = (bf16[64,3,1,256]{3,0,2,1:T(8,128)(2,1)S(1)}, bf16[64,3,1,256]{3,0,2,1:T(8,128)(2,1)S(1)}, u32[]{:S(2)}, u32[]{:S(2)}) collective-permute-start(bf16[64,3,1,256]{3,0,2,1:T(8,128)(2,1)S(1)} %copy.50), channel_id=1, source_target_pairs={{0,1},{2,3},{4,5},{6,7},{8,9},{10,11},{12,13},{14,15},{16,17},{18,... | collective-permute-start | bytes 294920 | tf_op jit(solution)/shard_map/ppermute | solution.py:19
  35.0 8.8 %copy-start.3 = (s32[4,4]{1,0:T(4,128)S(1)}, s32[4,4]{1,0:T(4,128)}, u32[]{:S(2)}) copy-start(s32[4,4]{1,0:T(4,128)} %param.16) | copy-start | bytes 196
  35.0 8.9 %copy-start.4 = (f32[4,4]{1,0:T(4,128)S(1)}, f32[4,4]{1,0:T(4,128)}, u32[]{:S(2)}) copy-start(f32[4,4]{1,0:T(4,128)} %param.17) | copy-start | bytes 196
  35.0 8.9 %copy-start.1 = (f32[4,32,64]{2,1,0:T(8,128)S(1)}, f32[4,32,64]{2,1,0:T(8,128)}, u32[]{:S(2)}) copy-start(f32[4,32,64]{2,1,0:T(8,128)} %param.15) | copy-start | bytes 98308
  35.0 223.4 %copy-start.2 = (s32[5,2]{0,1:T(2,128)S(1)}, s32[5,2]{0,1:T(2,128)}, u32[]{:S(2)}) copy-start(s32[5,2]{0,1:T(2,128)} %param.14) | copy-start | bytes 124
  35.0 223.4 %all-to-all-start = ((bf16[144,3,26,256]{3,2,1,0:T(8,128)(2,1)}), bf16[144,3,26,256]{3,2,1,0:T(8,128)(2,1)}, u32[]{:S(2)}, u32[]{:S(2)}) async-start(bf16[144,3,26,256]{3,2,1,0:T(8,128)(2,1)} %broadcast_select_fusion.1), calls=%async_computation | async-start | bytes 14155776 | tf_op jit(solution)/shard_map/all_to_all | solution.py:53
  43.5 213.9 %all-reduce.2.cloned.1.call-start = ((), (), s32[]{:S(2)}) async-start(), calls=%async_computation.1 | async-start | bytes 1310720 | tf_op jit(solution)/shard_map/psum | solution.py:71
  439.7 9.4 %copy-start = (bf16[5,3,32,4096]{3,2,1,0:T(8,128)(2,1)S(1)}, bf16[5,3,32,4096]{3,2,1,0:T(8,128)(2,1)}, u32[]{:S(2)}) copy-start(bf16[5,3,32,4096]{3,2,1,0:T(8,128)(2,1)} %get-tuple-element.138) | copy-start | bytes 11796484
  444.2 2.6 collective-permute-start.2
  445.5 3.3 collective-permute-start.3
Sparse Core Ops, SparseCore 0:
  49.7 207.6 all-reduce.1
where the time goes:
time: 489 us; the launch traced here: 488 us
  waiting for transfers between devices  213 us (44%)
  local copies, waits for them, and re-layouts  130 us (27%)
  matrix products  56.9 us (12%)
  other arithmetic  31.4 us (6%)
  loops' own time  26.5 us (5%)
  starting transfers between devices  15.7 us (3%)
  between operations  13.7 us (3%)
    psum x1, waiting for transfers between devices, body(): summed = lax.psum(partial_value, ('tile', 'box'))  212 us
    gather x10, local copies, waits for them, and re-layouts, one_box(): patch_tiles = jnp.take(incoming, box_ids, axis=0)  52.5 us
    dot_general x5, matrix products, one_box(): jnp.einsum('rscLyx,sxi->cLryi', patch_tiles, weights_x, preferred_element...  28.2 us
    another operation x1, loops' own time, body(): box_flow = lax.map(one_box, (flat_index, box_offset, wake_loss))  26.5 us
    convert_element_type x1, other arithmetic, body(): return (center + FILTER_NU * stencil_sum).astype(jnp.bfloat16)  15.3 us
    dot_general x5, matrix products, one_box(): jnp.einsum('cLp,Lk->ckp', along_y, height_weights, precision=lax.Precisio...  14.2 us
    dot_general x5, matrix products, one_box(): jnp.einsum('cLryi,ryj->cLji', along_x, weights_y, precision=lax.Precision...  13.1 us
    another operation x10, local copies, waits for them, and re-layouts  11.5 us
  transfers between devices with their start and end apart: 6, of which 2 were waited for; matrix products, arithmetic and copies ran while one was open for 1% of the time, Pallas kernels for 0%

commit v1 on v0

--- a/solution.py
+++ b/solution.py
@@ -68,7 +68,7 @@
     partial_value = jnp.dot(
         onehot, deficit_terms, precision=lax.Precision.HIGHEST, preferred_element_type=jnp.float32
     )
-    summed = lax.psum(partial_value, ("tile", "box"))
+    summed = jnp.sum(jax.lax.all_gather(partial_value, ("tile", "box")), axis=0)
     wake_loss = lax.dynamic_slice_in_dim(summed, my_index * box_count, box_count, 0)
     wake_loss = wake_loss.reshape(box_count, slab_points, BOXN)
     points = slab_index * slab_points + jnp.arange(slab_points, dtype=jnp.int32)

time: 489 us -> 517 us (1.057)
  waiting for transfers between devices: 213 us -> 235 us
    all_gather x0 -> x1, waiting for transfers between devices: none -> 228 us  [body(): summed = jnp.sum(jax.lax.all_gather(partial_value, ('tile', 'box')), axis=0)]
    psum x1 -> x0, waiting for transfers between devices: 212 us -> none  [body(): summed = lax.psum(partial_value, ('tile', 'box'))]
    all_to_all x1, waiting for transfers between devices: 0.01 us -> 5.66 us  [body(): lax.all_to_all(outgoing, ('tile', 'box'), split_axis=0, concat_axis=0, ti...]
  transfers between devices with their start and end apart: 6 -> 6, of which waited for: 2 -> 3; matrix products, arithmetic and copies ran while one was open for 1% -> 6% of each run, Pallas kernels for 0% -> 0%
where the time goes in v1:
time: 517 us; the launch traced here: 515 us
  waiting for transfers between devices  235 us (45%)
  local copies, waits for them, and re-layouts  131 us (25%)
  matrix products  56.9 us (11%)
  other arithmetic  36.2 us (7%)
  loops' own time  26.1 us (5%)
  starting transfers between devices  15.8 us (3%)
  between operations  13.7 us (3%)
    all_gather x1, waiting for transfers between devices, body(): summed = jnp.sum(jax.lax.all_gather(partial_value, ('tile', 'box')), axis=0)  228 us
    gather x10, local copies, waits for them, and re-layouts, one_box(): patch_tiles = jnp.take(incoming, box_ids, axis=0)  52.4 us
    dot_general x5, matrix products, one_box(): jnp.einsum('rscLyx,sxi->cLryi', patch_tiles, weights_x, preferred_element...  28.2 us
    another operation x1, loops' own time, body(): box_flow = lax.map(one_box, (flat_index, box_offset, wake_loss))  26.1 us
    convert_element_type x1, other arithmetic, body(): return (center + FILTER_NU * stencil_sum).astype(jnp.bfloat16)  15.3 us
    dot_general x5, matrix products, one_box(): jnp.einsum('cLp,Lk->ckp', along_y, height_weights, precision=lax.Precisio...  14.2 us
    dot_general x5, matrix products, one_box(): jnp.einsum('cLryi,ryj->cLji', along_x, weights_y, precision=lax.Precision...  13.1 us
    another operation x10, local copies, waits for them, and re-layouts  11.4 us
  transfers between devices with their start and end apart: 6, of which 3 were waited for; matrix products, arithmetic and copies ran while one was open for 6% of the time, Pallas kernels for 0%

profile of v1, /device:TPU:0, one launch (start us, length us, event | category | flops | bytes accessed | tf_op | source)
XLA Modules:
  0.0 515.2 jit_solution(15751070843197000830)
XLA Ops:
  19.5 3.9 pad_maximum_fusion
  23.4 8.9 %gather_fusion.1 = bf16[144,3,26,256]{3,2,1,0:T(8,128)(2,1)} fusion(bf16[64,3,26,256]{3,2,1,0:T(8,128)(2,1)S(1)} %pad_maximum_fusion, s32[1024]{0:T(1024)S(1)} %pad_clamp_fusion.1), kind=kCustom, calls=%fused_computation.1 | custom fusion | bytes 11502144 | tf_op jit(solution)/shard_map/jit(_take)/gather | solution.py:52
  32.3 6.6 %broadcast_select_fusion.1 = bf16[144,3,26,256]{3,2,1,0:T(8,128)(2,1)} fusion(bf16[144,3,26,256]{3,2,1,0:T(8,128)(2,1)} %gather_fusion.1, pred[144]{0:T(512)(128)(4,1)S(1)} %compare_and_fusion.1), kind=kLoop, calls=%fused_computation.74 | loop fusion | flops 2875392 | bytes 11501712 | tf_op jit(solution)/shard_map/jit(_take)/select_n | solution.py:52
  38.9 8.5 %all-to-all-start = ((bf16[144,3,26,256]{3,2,1,0:T(8,128)(2,1)}), bf16[144,3,26,256]{3,2,1,0:T(8,128)(2,1)}, u32[]{:S(2)}, u32[]{:S(2)}) async-start(bf16[144,3,26,256]{3,2,1,0:T(8,128)(2,1)} %broadcast_select_fusion.1), calls=%async_computation | async-start | bytes 14155776 | tf_op jit(solution)/shard_map/all_to_all | solution.py:53
  47.8 228.1 %all-gather.3.cloned.1.call-done = f32[1280,2048]{1,0:T(8,128)} async-done(((f32[80,2048]{1,0:T(8,128)}), f32[1280,2048]{1,0:T(8,128)}) %all-gather.3.cloned.1.call-update) | async-done | bytes 10485776 | tf_op jit(solution)/shard_map/all_gather | solution.py:71
  275.9 4.8 reduce_sum.32
  280.8 5.7 %all-to-all-done = bf16[144,3,26,256]{3,2,1,0:T(8,128)(2,1)} async-done(((bf16[144,3,26,256]{3,2,1,0:T(8,128)(2,1)}), bf16[144,3,26,256]{3,2,1,0:T(8,128)(2,1)}, u32[]{:S(2)}, u32[]{:S(2)}) %all-to-all-start) | async-done | bytes 5750816 | tf_op jit(solution)/shard_map/all_to_all | solution.py:53
  286.4 180.6 %while.15 = (s32[]{:T(128)}, bf16[5,3,32,4096]{3,2,1,0:T(8,128)(2,1)}, s32[5,2]{0,1:T(2,128)S(1)}, s32[5,25]{1,0:T(8,128)S(1)}, bf16[144,3,26,256]{3,2,1,0:T(8,1...) while((s32[]{:T(128)}, ...), condition=%wide.region_5.6_spmd.clone, body=%wide.region_4.5_spmd.clone.sunk | while | flops 493983968 | bytes 24612900 | solution.py:122
  292.4 3.6 gather_fusion
  296.1 6.8 %gather.24 = bf16[5,5,3,26,16,16]{5,4,3,2,1,0:T(8,128)(2,1)} reshape(bf16[25,3,26,256]{3,2,1,0:T(8,128)(2,1)S(1)} %gather_fusion) | data formatting | bytes 1996800 | tf_op jit(solution)/shard_map/while/body/eval_jaxpr/jit(_take)/gather | solution.py:90
  302.9 5.6 %fusion.96 = f32[64,5,3,26,16,1]{0,4,5,1,3,2:T(8,128)S(1)} fusion(f32[]{:T(128)S(6)} %div.72, s32[64]{0:T(128)S(1)} %get-tuple-element.283, f32[]{:T(128)S(6)} %sub.148, s32[64]{0:T(128)S(1)} %get-tuple-element.284, s32[5,16]{1,0:T(8,128)S(1)} %multiply_add_fusion.2, bf16[5,5,3,26,16,16]{5,4,3,2,1,0:T(8,128)(2,1)} %gather.24, ...), kind=kOutput, calls=%fused_computation.3.clone.1 | convolution fusion | flops 64427520 | bytes 2596705 | tf_op jit(solution)/shard_map/while/body/eval_jaxpr/rscLyx,sxi->cLryi/dot_general | solution.py:100
  332.2 6.8 %gather.24 = bf16[5,5,3,26,16,16]{5,4,3,2,1,0:T(8,128)(2,1)} reshape(bf16[25,3,26,256]{3,2,1,0:T(8,128)(2,1)S(1)} %gather_fusion) | data formatting | bytes 1996800 | tf_op jit(solution)/shard_map/while/body/eval_jaxpr/jit(_take)/gather | solution.py:90
  339.0 5.6 %fusion.96 = f32[64,5,3,26,16,1]{0,4,5,1,3,2:T(8,128)S(1)} fusion(f32[]{:T(128)S(6)} %div.72, s32[64]{0:T(128)S(1)} %get-tuple-element.283, f32[]{:T(128)S(6)} %sub.148, s32[64]{0:T(128)S(1)} %get-tuple-element.284, s32[5,16]{1,0:T(8,128)S(1)} %multiply_add_fusion.2, bf16[5,5,3,26,16,16]{5,4,3,2,1,0:T(8,128)(2,1)} %gather.24, ...), kind=kOutput, calls=%fused_computation.3.clone.1 | convolution fusion | flops 64427520 | bytes 2596705 | tf_op jit(solution)/shard_map/while/body/eval_jaxpr/rscLyx,sxi->cLryi/dot_general | solution.py:100
  368.3 6.8 %gather.24 = bf16[5,5,3,26,16,16]{5,4,3,2,1,0:T(8,128)(2,1)} reshape(bf16[25,3,26,256]{3,2,1,0:T(8,128)(2,1)S(1)} %gather_fusion) | data formatting | bytes 1996800 | tf_op jit(solution)/shard_map/while/body/eval_jaxpr/jit(_take)/gather | solution.py:90
  375.1 5.6 %fusion.96 = f32[64,5,3,26,16,1]{0,4,5,1,3,2:T(8,128)S(1)} fusion(f32[]{:T(128)S(6)} %div.72, s32[64]{0:T(128)S(1)} %get-tuple-element.283, f32[]{:T(128)S(6)} %sub.148, s32[64]{0:T(128)S(1)} %get-tuple-element.284, s32[5,16]{1,0:T(8,128)S(1)} %multiply_add_fusion.2, bf16[5,5,3,26,16,16]{5,4,3,2,1,0:T(8,128)(2,1)} %gather.24, ...), kind=kOutput, calls=%fused_computation.3.clone.1 | convolution fusion | flops 64427520 | bytes 2596705 | tf_op jit(solution)/shard_map/while/body/eval_jaxpr/rscLyx,sxi->cLryi/dot_general | solution.py:100
  404.4 6.8 %gather.24 = bf16[5,5,3,26,16,16]{5,4,3,2,1,0:T(8,128)(2,1)} reshape(bf16[25,3,26,256]{3,2,1,0:T(8,128)(2,1)S(1)} %gather_fusion) | data formatting | bytes 1996800 | tf_op jit(solution)/shard_map/while/body/eval_jaxpr/jit(_take)/gather | solution.py:90
  411.3 5.6 %fusion.96 = f32[64,5,3,26,16,1]{0,4,5,1,3,2:T(8,128)S(1)} fusion(f32[]{:T(128)S(6)} %div.72, s32[64]{0:T(128)S(1)} %get-tuple-element.283, f32[]{:T(128)S(6)} %sub.148, s32[64]{0:T(128)S(1)} %get-tuple-element.284, s32[5,16]{1,0:T(8,128)S(1)} %multiply_add_fusion.2, bf16[5,5,3,26,16,16]{5,4,3,2,1,0:T(8,128)(2,1)} %gather.24, ...), kind=kOutput, calls=%fused_computation.3.clone.1 | convolution fusion | flops 64427520 | bytes 2596705 | tf_op jit(solution)/shard_map/while/body/eval_jaxpr/rscLyx,sxi->cLryi/dot_general | solution.py:100
  436.9 3.6 gather_fusion
  440.5 6.8 %gather.24 = bf16[5,5,3,26,16,16]{5,4,3,2,1,0:T(8,128)(2,1)} reshape(bf16[25,3,26,256]{3,2,1,0:T(8,128)(2,1)S(1)} %gather_fusion) | data formatting | bytes 1996800 | tf_op jit(solution)/shard_map/while/body/eval_jaxpr/jit(_take)/gather | solution.py:90
  447.4 5.6 %fusion.96 = f32[64,5,3,26,16,1]{0,4,5,1,3,2:T(8,128)S(1)} fusion(f32[]{:T(128)S(6)} %div.72, s32[64]{0:T(128)S(1)} %get-tuple-element.283, f32[]{:T(128)S(6)} %sub.148, s32[64]{0:T(128)S(1)} %get-tuple-element.284, s32[5,16]{1,0:T(8,128)S(1)} %multiply_add_fusion.2, bf16[5,5,3,26,16,16]{5,4,3,2,1,0:T(8,128)(2,1)} %gather.24, ...), kind=kOutput, calls=%fused_computation.3.clone.1 | convolution fusion | flops 64427520 | bytes 2596705 | tf_op jit(solution)/shard_map/while/body/eval_jaxpr/rscLyx,sxi->cLryi/dot_general | solution.py:100
  467.1 4.5 copy.42
  478.8 7.1 %fusion.71 = (f32[5,3,32,4095]{3,2,1,0:T(8,128)}, f32[5,3,32,4095]{3,2,1,0:T(8,128)}) fusion(f32[5,3,34,4096]{3,2,1,0:T(8,128)S(1)} %maximum_convert_fusion), kind=kLoop, calls=%fused_computation.123 | loop fusion | bytes 31449600 | tf_op jit(solution)/shard_map/slice | solution.py:135
  485.9 7.1 %fusion.72 = (f32[5,3,32,4032]{3,2,1,0:T(8,128)}, f32[5,3,32,4032]{3,2,1,0:T(8,128)}) fusion(f32[5,3,34,4096]{3,2,1,0:T(8,128)S(1)} %maximum_convert_fusion), kind=kLoop, calls=%fused_computation.124 | loop fusion | bytes 30965760 | tf_op jit(solution)/shard_map/slice | solution.py:130
  493.0 15.3 %fusion.50 = bf16[5,3,32,4096]{3,2,1,0:T(8,128)(2,1)} fusion(f32[5,3,34,4096]{3,2,1,0:T(8,128)S(1)} %maximum_convert_fusion, f32[5,3,32,4032]{3,2,1,0:T(8,128)} %get-tuple-element.196, f32[5,3,32,64]{3,2,1,0:T(8,128)S(1)} %get-tuple-element.202, f32[5,3,32,64]{3,2,1,0:T(8,128)S(1)} %get-tuple-element.201, f32[5,3,32,4032]{3,2,1,0:T(8,128)} %get-tuple-element.195, ...), kind=kLoop, calls=%fused_computation.71 | loop fusion | flops 43253760 | bytes 58990656 | tf_op jit(solution)/shard_map/convert_element_type | solution.py:140
  (159 shorter events, 105.4 us)
Async XLA Ops:
  6.5 269.3 %all-gather.3.cloned.1.call-start = ((), (), s32[]{:S(2)}) async-start(), calls=%async_computation.1 | async-start | bytes 11141120 | tf_op jit(solution)/shard_map/all_gather | solution.py:71
  12.2 7.0 %collective-permute-start.1 = (bf16[64,3,1,256]{3,0,2,1:T(8,128)(2,1)S(1)}, bf16[64,3,1,256]{3,0,2,1:T(8,128)(2,1)S(1)}, u32[]{:S(2)}, u32[]{:S(2)}) collective-permute-start(bf16[64,3,1,256]{3,0,2,1:T(8,128)(2,1)S(1)} %copy.51), channel_id=1, source_target_pairs={{1,0},{3,2},{5,4},{7,6},{9,8},{11,10},{13,12},{15,14},{17,16},{19,... | collective-permute-start | bytes 294920 | tf_op jit(solution)/shard_map/ppermute | solution.py:20
  13.5 5.8 %collective-permute-start = (bf16[64,3,1,256]{3,0,2,1:T(8,128)(2,1)S(1)}, bf16[64,3,1,256]{3,0,2,1:T(8,128)(2,1)S(1)}, u32[]{:S(2)}, u32[]{:S(2)}) collective-permute-start(bf16[64,3,1,256]{3,0,2,1:T(8,128)(2,1)S(1)} %copy.50), channel_id=1, source_target_pairs={{0,1},{2,3},{4,5},{6,7},{8,9},{10,11},{12,13},{14,15},{16,17},{18,... | collective-permute-start | bytes 294920 | tf_op jit(solution)/shard_map/ppermute | solution.py:19
  38.9 247.6 %all-to-all-start = ((bf16[144,3,26,256]{3,2,1,0:T(8,128)(2,1)}), bf16[144,3,26,256]{3,2,1,0:T(8,128)(2,1)}, u32[]{:S(2)}, u32[]{:S(2)}) async-start(bf16[144,3,26,256]{3,2,1,0:T(8,128)(2,1)} %broadcast_select_fusion.1), calls=%async_computation | async-start | bytes 14155776 | tf_op jit(solution)/shard_map/all_to_all | solution.py:53
  47.4 239.1 %copy-start.1 = (s32[5,2]{0,1:T(2,128)S(1)}, s32[5,2]{0,1:T(2,128)}, u32[]{:S(2)}) copy-start(s32[5,2]{0,1:T(2,128)} %param.14) | copy-start | bytes 124
  467.1 9.8 %copy-start = (bf16[5,3,32,4096]{3,2,1,0:T(8,128)(2,1)S(1)}, bf16[5,3,32,4096]{3,2,1,0:T(8,128)(2,1)}, u32[]{:S(2)}) copy-start(bf16[5,3,32,4096]{3,2,1,0:T(8,128)(2,1)} %get-tuple-element.138) | copy-start | bytes 11796484
  471.6 3.0 collective-permute-start.2
  473.2 3.3 collective-permute-start.3
Sparse Core Ops, SparseCore 0:
  10.6 265.2 all-gather.2
